TPU v7x, 32 devices: a whole 2x2x4 slice. The times are simulated.
32 devices in a mesh: rotor: 4 (over y, core), blk: 8 (over z, x).
Axes of the slice: x: 2, y: 2, z: 4, core: 2. Of those that a mesh axis runs over, the one named last changes fastest.
Arguments:
- positions: float32 [3, 131072], P(None, ('rotor', 'blk')), may hold values from -6 to 6
- strengths: float32 [3, 131072], P(None, ('rotor', 'blk'))
- blade_of_block: int32 [1024], P(('rotor', 'blk')), may hold values from 0 to 29
- circulation: float32 [30], replicated, may hold values from 0.5 to 2
- tile_source_dev: int32 [8192, 1], P(('rotor', 'blk')), may hold values from 0 to 31; in each aligned block of 256 rows (0 to 255, 256 to 511, ...) at most 12 rows name the same one
- tile_source_blk: int32 [8192], P(('rotor', 'blk')), may hold values from 0 to 31
- tile_target: int32 [8192], P(('rotor', 'blk')), may hold values from 0 to 31
- tile_count: int32 [32], P(('rotor', 'blk')), may hold values from 128 to 256, as said below
Outputs:
- velocity: float32 [3, 131072], P(None, ('rotor', 'blk'))
- strength_rate: float32 [3, 131072], P(None, ('rotor', 'blk'))
Inputs may be any that keep to these rules, and one draw needn't show every extreme that they name: `tile_source_dev`: among the 256 slots of one device no device number appears more than 12 times, and one appears exactly 12 times. `tile_count`: some device has all 256 slots live.
All inputs are finite; a program needn't handle non-finite values.
Results may differ from a plain program's by a relative error of at most 0.0003.
Values sent between devices are 32-bit elements; how exact they have to be, the bound alone decides.
A program may use at most 128 MiB of HBM per device.

v0:
```python
import math
import jax
import jax.numpy as jnp
from jax import lax
from jax.sharding import PartitionSpec as P

inverse_four_pi = 1.0 / (4.0 * math.pi)
core_square = 1.0
diffusion_rate = 2.0
highest = lax.Precision.HIGHEST


def with_halo(cells, sides, width):
    for axis, dim in sides:
        count = lax.axis_size(axis)
        ends = count - 1
        head = lax.slice_in_dim(cells, 0, width, axis=dim)
        tail = lax.slice_in_dim(cells, cells.shape[dim] - width, cells.shape[dim], axis=dim)
        cells = jnp.concatenate(
            [
                lax.ppermute(tail, axis, [(i, (i + 1) % count) for i in range(ends)]),
                cells,
                lax.ppermute(head, axis, [((i + 1) % count, i) for i in range(ends)]),
            ],
            axis=dim,
        )
    return cells


def cross_rows(left, right):
    return jnp.stack(
        [
            left[1] * right[2] - left[2] * right[1],
            left[2] * right[0] - left[0] * right[2],
            left[0] * right[1] - left[1] * right[0],
        ]
    )


def contract(matrix, values):
    return jnp.einsum("ts,cs->ct", matrix, values, precision=highest)


def kernels(target_pos, source_pos):
    offset_vec = target_pos[:, :, None] - source_pos[:, None, :]
    distance_sq = jnp.sum(offset_vec * offset_vec, axis=0)
    inverse = 1.0 / (distance_sq + core_square)
    green_kernel = inverse_four_pi * inverse * jnp.sqrt(inverse)
    return (green_kernel, 3.0 * green_kernel * inverse, jnp.exp(-distance_sq / core_square))


def toward(target, source, green_kernel, hessian, smooth):
    target_pos, target_str = (target[:3], target[3:])
    source_pos, source_str = (source[:3], source[3:])
    spin_src = cross_rows(source_pos, source_str)
    green_str = contract(green_kernel, source_str)
    velocity = contract(green_kernel, spin_src) - cross_rows(target_pos, green_str)
    along_axis = jnp.sum(target_str * target_pos, axis=0)[:, None] - jnp.einsum(
        "ct,cs->ts", target_str, source_pos, precision=highest
    )
    lever_arm = hessian * along_axis
    stretch = (
        cross_rows(target_pos, contract(lever_arm, source_str))
        - contract(lever_arm, spin_src)
        - cross_rows(target_str, green_str)
    )
    diffusion = contract(smooth, source_str) - jnp.sum(smooth, axis=1)[None, :] * target_str
    return jnp.concatenate([velocity, stretch + diffusion_rate * diffusion], axis=0)


def near_block(target, sources, validity):
    green_kernel, hessian, smooth = kernels(target[:3], sources[:3])
    return toward(target, sources, green_kernel, hessian, smooth * validity[None, :])


def tile_pair(target, source):
    green_kernel, hessian, smooth = kernels(target[:3], source[:3])
    forward = toward(target, source, green_kernel, hessian, smooth)
    backward = toward(source, target, green_kernel.T, hessian.T, smooth.T)
    return (forward, backward)


def send_requests(request):
    return lax.all_to_all(request, ("rotor", "blk"), split_axis=0, concat_axis=0, tiled=True)


def send_blocks(outgoing):
    return lax.all_to_all(outgoing, ("rotor", "blk"), split_axis=0, concat_axis=0, tiled=True)


def send_results(results):
    return lax.all_to_all(results, ("rotor", "blk"), split_axis=0, concat_axis=0, tiled=True)


def local(
    positions,
    strengths,
    blade_of_block,
    circulation,
    tile_source_dev,
    tile_source_blk,
    tile_target,
    tile_count,
):
    local_blocks = blade_of_block.shape[0]
    width = positions.shape[1] // local_blocks
    n_rotor = lax.axis_size("rotor")
    n_blk = lax.axis_size("blk")
    devices = n_rotor * n_blk
    magnitude = (
        jnp.sqrt(jnp.sum(strengths * strengths, axis=0)).reshape(local_blocks, width).sum(axis=1)
    )
    member = (
        blade_of_block[:, None] == jnp.arange(circulation.shape[0], dtype=jnp.int32)[None, :]
    ).astype(jnp.float32)
    totals, counted = lax.psum(
        (jnp.sum(member * magnitude[:, None], axis=0), jnp.sum(member, axis=0) * width),
        ("rotor", "blk"),
    )
    factor = circulation / (totals / jnp.maximum(counted, 1.0) + 1e-06)
    block_factor = jnp.sum(member * factor[None, :], axis=1)
    scaled = strengths * jnp.repeat(block_factor, width)[None, :]
    state = jnp.concatenate([positions, scaled], axis=0)
    blocks = state.reshape(6, local_blocks, width).transpose(1, 0, 2)
    padded = with_halo(state, (("blk", 1),), width)
    place = lax.axis_index("blk")
    validity = jnp.concatenate(
        [
            jnp.full((width,), place > 0),
            jnp.ones((local_blocks * width,), bool),
            jnp.full((width,), place < n_blk - 1),
        ]
    ).astype(jnp.float32)

    def near_one(index):
        start = index * width
        sources = lax.dynamic_slice_in_dim(padded, start, 3 * width, 1)
        weights = lax.dynamic_slice_in_dim(validity, start, 3 * width, 0)
        return near_block(blocks[index], sources, weights)

    near_group = math.gcd(local_blocks, 16)
    near = lax.map(
        jax.vmap(near_one), jnp.arange(local_blocks, dtype=jnp.int32).reshape(-1, near_group)
    )
    near = near.reshape(local_blocks, 6, width)
    capacity = tile_target.shape[0]
    slot_count = max(2, (3 * capacity + 2 * devices - 1) // (2 * devices))
    source_dev = tile_source_dev[:, 0]
    positions_idx = jnp.arange(capacity, dtype=jnp.int32)
    live_tile = (positions_idx < tile_count[0]).astype(jnp.float32)
    same_peer = (source_dev[:, None] == source_dev[None, :]) & (
        positions_idx[:, None] > positions_idx[None, :]
    )
    rank_in_peer = jnp.sum(same_peer.astype(jnp.int32), axis=1)
    slot_index = source_dev * slot_count + rank_in_peer
    wanted = (
        slot_index[None, :] == jnp.arange(devices * slot_count, dtype=jnp.int32)[:, None]
    ).astype(jnp.int32)
    request = (jnp.sum(wanted * (tile_source_blk[None, :] + 1), axis=1) - 1).reshape(
        devices, slot_count
    )
    asked = send_requests(request)
    present = (asked >= 0).astype(jnp.float32)
    outgoing = blocks[jnp.clip(asked, 0, local_blocks - 1)] * present[:, :, None, None]
    incoming = send_blocks(outgoing)
    sources = incoming.reshape(devices * slot_count, 6, width)[slot_index]
    targets = blocks[tile_target]
    tile_batch = math.gcd(capacity, 64)
    groups = capacity // tile_batch

    def tile_group(pair):
        return jax.vmap(tile_pair)(pair[0], pair[1])

    target_out, source_out = lax.map(
        tile_group,
        (
            targets.reshape(groups, tile_batch, 6, width),
            sources.reshape(groups, tile_batch, 6, width),
        ),
    )
    target_out = target_out.reshape(capacity, 6, width) * live_tile[:, None, None]
    source_out = source_out.reshape(capacity, 6, width) * live_tile[:, None, None]
    target_hot = (
        tile_target[None, :] == jnp.arange(local_blocks, dtype=jnp.int32)[:, None]
    ).astype(jnp.float32)
    cross_target = jnp.einsum("nc,cxp->nxp", target_hot, target_out, precision=highest)
    back = jnp.einsum("fc,cxp->fxp", wanted.astype(jnp.float32), source_out, precision=highest)
    returned = send_results(back.reshape(devices, slot_count, 6, width))
    return_hot = (
        asked.reshape(-1)[None, :] == jnp.arange(local_blocks, dtype=jnp.int32)[:, None]
    ).astype(jnp.float32)
    cross_source = jnp.einsum(
        "nf,fxp->nxp",
        return_hot,
        returned.reshape(devices * slot_count, 6, width),
        precision=highest,
    )
    total = near + cross_target + cross_source
    flat_terms = total.transpose(1, 0, 2).reshape(6, local_blocks * width)
    return (flat_terms[:3], flat_terms[3:])


def solution(mesh):
    placed = (
        P(None, ("rotor", "blk")),
        P(None, ("rotor", "blk")),
        P(("rotor", "blk")),
        P(),
        P(("rotor", "blk"), None),
        P(("rotor", "blk")),
        P(("rotor", "blk")),
        P(("rotor", "blk")),
    )
    return jax.shard_map(
        local,
        mesh=mesh,
        in_specs=placed,
        out_specs=(P(None, ("rotor", "blk")), P(None, ("rotor", "blk"))),
        check_vma=False,
    )
```

profile of v0, /device:TPU:0, one launch (start us, length us, event | category | flops | bytes accessed | tf_op | source)
XLA Modules:
  0.0 721.0 jit_solution(6770685092090512786)
XLA Ops:
  3.7 7.3 %all-to-all-start = ((s32[32,1,12]{2,1,0:T(1,128)}), s32[32,1,12]{2,1,0:T(1,128)S(1)}, u32[]{:S(2)}, u32[]{:S(2)}) async-start(s32[32,1,12]{2,1,0:T(1,128)} %bitcast.65), calls=%async_computation | async-start | bytes 32768 | tf_op jit(solution)/shard_map/all_to_all | solution.py:84
  12.7 40.5 %all-reduce.2 = (f32[30]{0:T(128)S(1)}, f32[30]{0:T(128)S(1)}) all-reduce(f32[30]{0:T(128)S(1)} %get-tuple-element.104, f32[30]{0:T(128)S(1)} %broadcast_multiply_fusion.4), channel_id=1, replica_groups=mesh['rotor'=4,'blk'=8] {'rotor','blk'}, use_global_device_ids=true, to_apply=%region_3.0 | all-reduce | flops 60 | bytes 480 | tf_op jit(solution)/shard_map/psum | solution.py:116
  61.6 4.5 all-to-all-start.1
  66.7 4.3 collective-permute-start
  79.8 25.1 %all-to-all-done.1 = f32[32,12,6,128]{3,2,1,0:T(8,128)S(1)} async-done(((f32[32,12,6,128]{3,2,1,0:T(8,128)}), f32[32,12,6,128]{3,2,1,0:T(8,128)S(1)}, u32[]{:S(2)}, u32[]{:S(2)}) %all-to-all-start.1) | async-done | bytes 1179680 | tf_op jit(solution)/shard_map/all_to_all | solution.py:88
  107.1 416.8 %while.29 = (s32[]{:T(128)}, f32[4,64,6,128]{3,1,0,2:T(8,128)}, f32[4,64,6,128]{3,1,0,2:T(8,128)}, f32[4,64,6,128]{3,1,2,0:T(8,128)}, f32[4,64,6,128]{3,1,2,0:T(8,128)S(1)}, /*index=5*/s32[]{:T(128)}) while((s32[]{:T(128)}, f32[4,64,6,128]{3,1,0,2:T(8,128)}, f32[4,64,6,128]{3,1,0,2:T(8,128)}, f32[4,64,6,128]{3,1,2,0:T(8,128)}, ...), condition=%wide.region_20.21_spmd, body=%wide.region_14.20_spmd.sunk | while | flops 495419392 | bytes 144605344 | solution.py:174
  108.5 4.1 multiply_reduce_fusion.13
  116.2 6.6 fusion.211
  122.8 8.4 %fusion.214 = f32[64,128,128]{1,2,0:T(8,128)S(1)} fusion(f32[64,128]{1,0:T(8,128)S(1)} %get-tuple-element.490, f32[64,3,128]{2,0,1:T(8,128)S(1)} %get-tuple-element.473, f32[64,3,128]{2,0,1:T(8,128)S(1)} %get-tuple-element.469, f32[64,128,128]{2,1,0:T(8,128)S(1)} %multiply_reduce_fusion.13), kind=kOutput, calls=%fused_computation.10.clone.1 | convolution fusion | flops 46137344 | bytes 8617984 | tf_op jit(solution)/shard_map/while/body/eval_jaxpr/vmap(ct,cs->ts)/dot_general | solution.py:58
  142.0 5.6 copy.502
  147.6 9.2 %fusion.224 = f32[64,3,128]{2,1,0:T(4,128)S(1)} fusion(f32[64,128,128]{1,2,0:T(8,128)} %copy.502, f32[3,64,128]{2,1,0:T(8,128)S(1)} %pad_maximum_fusion.18), kind=kOutput, calls=%fused_computation.21.clone.1 | convolution fusion | flops 39845888 | bytes 4390912 | tf_op jit(solution)/shard_map/while/body/eval_jaxpr/vmap(ts,cs->ct)/dot_general | solution.py:41
  156.8 7.2 fusion.212
  164.0 4.5 fusion.209
  168.7 4.7 fusion.219
  176.8 5.6 copy.503
  182.4 10.4 %subtract_multiply_fusion.5 = f32[64,128,128]{2,1,0:T(8,128)S(1)} fusion(f32[64,128,128]{2,1,0:T(8,128)} %copy.503, f32[64,128]{1,0:T(8,128)S(1)} %get-tuple-element.471, f32[64,3,128]{2,0,1:T(8,128)S(1)} %get-tuple-element.472, f32[64,3,128]{2,0,1:T(8,128)S(1)} %get-tuple-element.468, f32[64,128,128]{2,1,0:T(8,128)} %copy-done.1), kind=kOutput, calls=%fused_computation.12.clone.1 | convolution fusion | flops 42991616 | bytes 12812288 | tf_op jit(solution)/shard_map/while/body/eval_jaxpr/vmap(ct,cs->ts)/dot_general | solution.py:58
  192.9 6.6 fusion.217
  199.4 6.6 fusion.207
  208.4 4.1 multiply_reduce_fusion.13
  216.1 6.6 fusion.211
  222.7 8.4 %fusion.214 = f32[64,128,128]{1,2,0:T(8,128)S(1)} fusion(f32[64,128]{1,0:T(8,128)S(1)} %get-tuple-element.490, f32[64,3,128]{2,0,1:T(8,128)S(1)} %get-tuple-element.473, f32[64,3,128]{2,0,1:T(8,128)S(1)} %get-tuple-element.469, f32[64,128,128]{2,1,0:T(8,128)S(1)} %multiply_reduce_fusion.13), kind=kOutput, calls=%fused_computation.10.clone.1 | convolution fusion | flops 46137344 | bytes 8617984 | tf_op jit(solution)/shard_map/while/body/eval_jaxpr/vmap(ct,cs->ts)/dot_general | solution.py:58
  241.9 5.6 copy.502
  247.5 9.2 %fusion.224 = f32[64,3,128]{2,1,0:T(4,128)S(1)} fusion(f32[64,128,128]{1,2,0:T(8,128)} %copy.502, f32[3,64,128]{2,1,0:T(8,128)S(1)} %pad_maximum_fusion.18), kind=kOutput, calls=%fused_computation.21.clone.1 | convolution fusion | flops 39845888 | bytes 4390912 | tf_op jit(solution)/shard_map/while/body/eval_jaxpr/vmap(ts,cs->ct)/dot_general | solution.py:41
  256.7 7.2 fusion.212
  263.9 4.5 fusion.209
  268.6 4.7 fusion.219
  276.7 5.6 copy.503
  282.3 10.4 %subtract_multiply_fusion.5 = f32[64,128,128]{2,1,0:T(8,128)S(1)} fusion(f32[64,128,128]{2,1,0:T(8,128)} %copy.503, f32[64,128]{1,0:T(8,128)S(1)} %get-tuple-element.471, f32[64,3,128]{2,0,1:T(8,128)S(1)} %get-tuple-element.472, f32[64,3,128]{2,0,1:T(8,128)S(1)} %get-tuple-element.468, f32[64,128,128]{2,1,0:T(8,128)} %copy-done.1), kind=kOutput, calls=%fused_computation.12.clone.1 | convolution fusion | flops 42991616 | bytes 12812288 | tf_op jit(solution)/shard_map/while/body/eval_jaxpr/vmap(ct,cs->ts)/dot_general | solution.py:58
  292.7 6.6 fusion.217
  299.3 6.6 fusion.207
  308.3 4.1 multiply_reduce_fusion.13
  315.9 6.6 fusion.211
  322.5 8.4 %fusion.214 = f32[64,128,128]{1,2,0:T(8,128)S(1)} fusion(f32[64,128]{1,0:T(8,128)S(1)} %get-tuple-element.490, f32[64,3,128]{2,0,1:T(8,128)S(1)} %get-tuple-element.473, f32[64,3,128]{2,0,1:T(8,128)S(1)} %get-tuple-element.469, f32[64,128,128]{2,1,0:T(8,128)S(1)} %multiply_reduce_fusion.13), kind=kOutput, calls=%fused_computation.10.clone.1 | convolution fusion | flops 46137344 | bytes 8617984 | tf_op jit(solution)/shard_map/while/body/eval_jaxpr/vmap(ct,cs->ts)/dot_general | solution.py:58
  341.7 5.6 copy.502
  347.3 9.2 %fusion.224 = f32[64,3,128]{2,1,0:T(4,128)S(1)} fusion(f32[64,128,128]{1,2,0:T(8,128)} %copy.502, f32[3,64,128]{2,1,0:T(8,128)S(1)} %pad_maximum_fusion.18), kind=kOutput, calls=%fused_computation.21.clone.1 | convolution fusion | flops 39845888 | bytes 4390912 | tf_op jit(solution)/shard_map/while/body/eval_jaxpr/vmap(ts,cs->ct)/dot_general | solution.py:41
  356.5 7.2 fusion.212
  363.8 4.5 fusion.209
  368.5 4.7 fusion.219
  376.5 5.6 copy.503
  382.2 10.4 %subtract_multiply_fusion.5 = f32[64,128,128]{2,1,0:T(8,128)S(1)} fusion(f32[64,128,128]{2,1,0:T(8,128)} %copy.503, f32[64,128]{1,0:T(8,128)S(1)} %get-tuple-element.471, f32[64,3,128]{2,0,1:T(8,128)S(1)} %get-tuple-element.472, f32[64,3,128]{2,0,1:T(8,128)S(1)} %get-tuple-element.468, f32[64,128,128]{2,1,0:T(8,128)} %copy-done.1), kind=kOutput, calls=%fused_computation.12.clone.1 | convolution fusion | flops 42991616 | bytes 12812288 | tf_op jit(solution)/shard_map/while/body/eval_jaxpr/vmap(ct,cs->ts)/dot_general | solution.py:58
  392.6 6.6 fusion.217
  399.2 6.6 fusion.207
  415.8 6.6 fusion.211
  422.4 8.4 %fusion.214 = f32[64,128,128]{1,2,0:T(8,128)S(1)} fusion(f32[64,128]{1,0:T(8,128)S(1)} %get-tuple-element.490, f32[64,3,128]{2,0,1:T(8,128)S(1)} %get-tuple-element.473, f32[64,3,128]{2,0,1:T(8,128)S(1)} %get-tuple-element.469, f32[64,128,128]{2,1,0:T(8,128)S(1)} %multiply_reduce_fusion.13), kind=kOutput, calls=%fused_computation.10.clone.1 | convolution fusion | flops 46137344 | bytes 8617984 | tf_op jit(solution)/shard_map/while/body/eval_jaxpr/vmap(ct,cs->ts)/dot_general | solution.py:58
  441.6 5.6 copy.502
  447.2 9.2 %fusion.224 = f32[64,3,128]{2,1,0:T(4,128)S(1)} fusion(f32[64,128,128]{1,2,0:T(8,128)} %copy.502, f32[3,64,128]{2,1,0:T(8,128)S(1)} %pad_maximum_fusion.18), kind=kOutput, calls=%fused_computation.21.clone.1 | convolution fusion | flops 39845888 | bytes 4390912 | tf_op jit(solution)/shard_map/while/body/eval_jaxpr/vmap(ts,cs->ct)/dot_general | solution.py:41
  456.4 7.2 fusion.212
  463.6 4.5 fusion.209
  468.3 4.7 fusion.219
  476.4 5.6 copy.503
  482.0 10.4 %subtract_multiply_fusion.5 = f32[64,128,128]{2,1,0:T(8,128)S(1)} fusion(f32[64,128,128]{2,1,0:T(8,128)} %copy.503, f32[64,128]{1,0:T(8,128)S(1)} %get-tuple-element.471, f32[64,3,128]{2,0,1:T(8,128)S(1)} %get-tuple-element.472, f32[64,3,128]{2,0,1:T(8,128)S(1)} %get-tuple-element.468, f32[64,128,128]{2,1,0:T(8,128)} %copy-done.1), kind=kOutput, calls=%fused_computation.12.clone.1 | convolution fusion | flops 42991616 | bytes 12812288 | tf_op jit(solution)/shard_map/while/body/eval_jaxpr/vmap(ct,cs->ts)/dot_general | solution.py:58
  492.5 6.6 fusion.217
  499.0 6.6 fusion.207
  531.9 186.4 %while.28 = (s32[]{:T(128)}, f32[2,16,6,128]{3,1,0,2:T(8,128)S(1)}, s32[2,16]{1,0:T(2,128)S(1)}, f32[6,4352]{1,0:T(8,128)}, f32[32,6,128]{2,1,0:T(8,128)S(1)}, /...) while((s32[]{:T(128)}, f32[2,16,6,128]{3,1,0,2:T(8,128)S(1)}, ...), condition=%wide.region_11.12_spmd, body=%wide.region_7.11_spmd.sunk | while | flops 192960656 | bytes 30571508 | solution.py:142
  531.9 32.7 %while.31 = (s32[]{:T(128)}, f32[4352]{0:T(1024)}, s32[16,1]{0,1:T(1,128)S(1)}, f32[16,384]{1,0:T(8,128)S(1)}, s32[]{:T(128)}, /*index=5*/s32[]{:T(128)}) while((s32[]{:T(128)}, f32[4352]{0:T(1024)}, s32[16,1]{0,1:T(1,128)S(1)}, f32[16,384]{1,0:T(8,128)S(1)}, s32[]{:T(128)}, /*index=5*/s32[]{:T(128)}) %tuple.176), condition=%wide.while_cond.1, body=%wide.while_body.1.sunk | while | flops 2 | bytes 9313 | solution.py:138
  565.3 32.7 %while.30 = (s32[]{:T(128)}, f32[6,4352]{1,0:T(8,128)}, s32[16,2]{0,1:T(2,128)S(1)}, f32[16,6,384]{2,1,0:T(8,128)S(1)}, s32[]{:T(128)}) while((s32[]{:T(128)}, f32[6,4352]{1,0:T(8,128)}, s32[16,2]{0,1:T(2,128)S(1)}, f32[16,6,384]{2,1,0:T(8,128)S(1)}, s32[]{:T(128)}) %tuple.173), condition=%wide.while_cond, body=%wide.while_body.sunk | while | flops 2 | bytes 21609 | solution.py:137
  600.3 4.5 fusion.180
  604.8 5.2 subtract_multiply_fusion.4
  620.5 4.5 fusion.188
  625.1 32.7 %while.31 = (s32[]{:T(128)}, f32[4352]{0:T(1024)}, s32[16,1]{0,1:T(1,128)S(1)}, f32[16,384]{1,0:T(8,128)S(1)}, s32[]{:T(128)}, /*index=5*/s32[]{:T(128)}) while((s32[]{:T(128)}, f32[4352]{0:T(1024)}, s32[16,1]{0,1:T(1,128)S(1)}, f32[16,384]{1,0:T(8,128)S(1)}, s32[]{:T(128)}, /*index=5*/s32[]{:T(128)}) %tuple.176), condition=%wide.while_cond.1, body=%wide.while_body.1.sunk | while | flops 2 | bytes 9313 | solution.py:138
  658.5 32.7 %while.30 = (s32[]{:T(128)}, f32[6,4352]{1,0:T(8,128)}, s32[16,2]{0,1:T(2,128)S(1)}, f32[16,6,384]{2,1,0:T(8,128)S(1)}, s32[]{:T(128)}) while((s32[]{:T(128)}, f32[6,4352]{1,0:T(8,128)}, s32[16,2]{0,1:T(2,128)S(1)}, f32[16,6,384]{2,1,0:T(8,128)S(1)}, s32[]{:T(128)}) %tuple.173), condition=%wide.while_cond, body=%wide.while_body.sunk | while | flops 2 | bytes 21609 | solution.py:137
  693.4 4.5 fusion.180
  698.0 5.2 subtract_multiply_fusion.4
  713.7 4.5 fusion.188
  (478 shorter events, 274.9 us)
Async XLA Ops:
  2.3 0.5 copy-start.10
  3.7 53.0 %all-to-all-start = ((s32[32,1,12]{2,1,0:T(1,128)}), s32[32,1,12]{2,1,0:T(1,128)S(1)}, u32[]{:S(2)}, u32[]{:S(2)}) async-start(s32[32,1,12]{2,1,0:T(1,128)} %bitcast.65), calls=%async_computation | async-start | bytes 32768 | tf_op jit(solution)/shard_map/all_to_all | solution.py:84
  55.7 10.3 %copy-start.4 = (f32[3,4096]{1,0:T(4,128)}, f32[3,4096]{1,0:T(4,128)S(1)}, u32[]{:S(2)}) copy-start(f32[3,4096]{1,0:T(4,128)S(1)} %broadcast_multiply_fusion.3) | copy-start | bytes 147460
  56.6 19.8 %copy-start.2 = (f32[32,6,128]{2,1,0:T(8,128)}, f32[32,6,128]{2,1,0:T(8,128)S(1)}, u32[]{:S(2)}) copy-start(f32[32,6,128]{2,1,0:T(8,128)S(1)} %fusion.88) | copy-start | bytes 294916
  58.0 8.1 %copy-start.6 = (f32[3,4096]{1,0:T(4,128)S(1)}, f32[3,4096]{1,0:T(4,128)}, u32[]{:S(2)}) copy-start(f32[3,4096]{1,0:T(4,128)} %param.12) | copy-start | bytes 147460
  58.0 16.0 %copy-start.15 = (s32[256]{0:T(256)S(1)}, s32[256]{0:T(256)}, u32[]{:S(2)}) copy-start(s32[256]{0:T(256)} %param.18) | copy-start | bytes 3076
  58.0 16.0 %copy-start.9 = (s32[256,1]{0,1:T(1,128)S(1)}, s32[256,1]{0,1:T(1,128)}, u32[]{:S(2)}) copy-start(s32[256,1]{0,1:T(1,128)} %param.16) | copy-start | bytes 3076
  61.6 43.3 %all-to-all-start.1 = ((f32[32,12,6,128]{3,2,1,0:T(8,128)}), f32[32,12,6,128]{3,2,1,0:T(8,128)S(1)}, u32[]{:S(2)}, u32[]{:S(2)}) async-start(f32[32,12,6,128]{3,2,1,0:T(8,128)} %broadcast_multiply_fusion.1), calls=%async_computation.1 | async-start | bytes 3145728 | tf_op jit(solution)/shard_map/all_to_all | solution.py:88
  66.7 11.6 %collective-permute-start = (f32[6,128]{1,0:T(8,128)}, f32[6,128]{1,0:T(8,128)}, u32[]{:S(2)}, u32[]{:S(2)}) collective-permute-start(f32[6,128]{1,0:T(8,128)} %get-tuple-element.226), channel_id=1, source_target_pairs={{0,1},{1,2},{2,3},{3,4},{4,5},{5,6},{6,7},{8,9},{9,10},{10,11},{11... | collective-permute-start | bytes 9224 | tf_op jit(solution)/shard_map/ppermute | solution.py:21
  70.9 7.3 %collective-permute-start.1 = (f32[6,128]{1,0:T(8,128)}, f32[6,128]{1,0:T(8,128)}, u32[]{:S(2)}, u32[]{:S(2)}) collective-permute-start(f32[6,128]{1,0:T(8,128)} %get-tuple-element.227), channel_id=1, source_target_pairs={{1,0},{2,1},{3,2},{4,3},{5,4},{6,5},{7,6},{9,8},{10,9},{11,10},{12... | collective-permute-start | bytes 9224 | tf_op jit(solution)/shard_map/ppermute | solution.py:23
  107.1 416.9 %copy-start.13 = (f32[4,64]{1,0:T(4,128)S(1)}, f32[4,64]{1,0:T(4,128)}, u32[]{:S(2)}) copy-start(f32[4,64]{1,0:T(4,128)} %fusion.97) | copy-start | bytes 3076
  107.1 418.2 %copy-start.8 = (s32[32,12]{0,1:T(8,128)S(1)}, s32[32,12]{0,1:T(8,128)}, u32[]{:S(2)}) copy-start(s32[32,12]{0,1:T(8,128)} %multiply_add_fusion) | copy-start | bytes 4612
  107.1 418.2 %copy-start.11 = (s32[256]{0:T(256)S(1)}, s32[256]{0:T(256)}, u32[]{:S(2)}) copy-start(s32[256]{0:T(256)} %copy-done.10) | copy-start | bytes 3076
  112.7 26.1 %copy-start.1 = (f32[64,128,128]{2,1,0:T(8,128)}, f32[64,128,128]{2,1,0:T(8,128)S(1)}, u32[]{:S(2)}) copy-start(f32[64,128,128]{2,1,0:T(8,128)S(1)} %multiply_reduce_fusion.13) | copy-start | bytes 12582916 | tf_op jit(solution)/shard_map/while
  147.6 9.2 %copy-start = (f32[64,128,128]{1,2,0:T(8,128)S(1)}, f32[64,128,128]{1,2,0:T(8,128)}, u32[]{:S(2)}) copy-start(f32[64,128,128]{1,2,0:T(8,128)} %copy.502) | copy-start | bytes 12582916 | tf_op jit(solution)/shard_map/while
  212.5 26.1 %copy-start.1 = (f32[64,128,128]{2,1,0:T(8,128)}, f32[64,128,128]{2,1,0:T(8,128)S(1)}, u32[]{:S(2)}) copy-start(f32[64,128,128]{2,1,0:T(8,128)S(1)} %multiply_reduce_fusion.13) | copy-start | bytes 12582916 | tf_op jit(solution)/shard_map/while
  247.5 9.2 %copy-start = (f32[64,128,128]{1,2,0:T(8,128)S(1)}, f32[64,128,128]{1,2,0:T(8,128)}, u32[]{:S(2)}) copy-start(f32[64,128,128]{1,2,0:T(8,128)} %copy.502) | copy-start | bytes 12582916 | tf_op jit(solution)/shard_map/while
  312.4 26.1 %copy-start.1 = (f32[64,128,128]{2,1,0:T(8,128)}, f32[64,128,128]{2,1,0:T(8,128)S(1)}, u32[]{:S(2)}) copy-start(f32[64,128,128]{2,1,0:T(8,128)S(1)} %multiply_reduce_fusion.13) | copy-start | bytes 12582916 | tf_op jit(solution)/shard_map/while
  347.3 9.2 %copy-start = (f32[64,128,128]{1,2,0:T(8,128)S(1)}, f32[64,128,128]{1,2,0:T(8,128)}, u32[]{:S(2)}) copy-start(f32[64,128,128]{1,2,0:T(8,128)} %copy.502) | copy-start | bytes 12582916 | tf_op jit(solution)/shard_map/while
  412.2 26.1 %copy-start.1 = (f32[64,128,128]{2,1,0:T(8,128)}, f32[64,128,128]{2,1,0:T(8,128)S(1)}, u32[]{:S(2)}) copy-start(f32[64,128,128]{2,1,0:T(8,128)S(1)} %multiply_reduce_fusion.13) | copy-start | bytes 12582916 | tf_op jit(solution)/shard_map/while
  447.2 9.2 %copy-start = (f32[64,128,128]{1,2,0:T(8,128)S(1)}, f32[64,128,128]{1,2,0:T(8,128)}, u32[]{:S(2)}) copy-start(f32[64,128,128]{1,2,0:T(8,128)} %copy.502) | copy-start | bytes 12582916 | tf_op jit(solution)/shard_map/while
  525.3 6.5 copy-start.3
  525.3 6.5 copy-start.7
  525.3 6.5 copy-start.14
  528.4 190.5 %all-to-all-start.2 = ((f32[32,12,6,128]{3,2,1,0:T(8,128)}), f32[32,12,6,128]{3,2,1,0:T(8,128)S(1)}, u32[]{:S(2)}, u32[]{:S(2)}) async-start(f32[32,12,6,128]{3,2,1,0:T(8,128)} %copy.348), calls=%async_computation.2 | async-start | bytes 3145728 | tf_op jit(solution)/shard_map/all_to_all | solution.py:92
  531.8 186.4 %copy-start.5 = (f32[4,64,6,128]{3,1,0,2:T(8,128)S(1)}, f32[4,64,6,128]{3,1,0,2:T(8,128)}, u32[]{:S(2)}) copy-start(f32[4,64,6,128]{3,1,0,2:T(8,128)} %get-tuple-element.63) | copy-start | bytes 2359300
  531.8 186.4 %copy-start.17 = (f32[256]{0:T(256)S(1)}, f32[256]{0:T(256)}, u32[]{:S(2)}) copy-start(f32[256]{0:T(256)} %compare_convert_fusion.1) | copy-start | bytes 3076
  531.9 186.5 %copy-start.16 = (s32[256]{0:T(256)S(1)}, s32[256]{0:T(256)}, u32[]{:S(2)}) copy-start(s32[256]{0:T(256)} %param.18) | copy-start | bytes 3076
  531.9 187.0 %copy-start.12 = (s32[384]{0:T(512)S(1)}, s32[384]{0:T(512)}, u32[]{:S(2)}) copy-start(s32[384]{0:T(512)} %eq.96) | copy-start | bytes 4612
where the time goes:
time: 731 us; the launch traced here: 721 us
  matrix products  352 us (48%)
  local copies, waits for them, and re-layouts  193 us (26%)
  other arithmetic  67.8 us (9%)
  blocking collectives  40.5 us (6%)
  waiting for transfers between devices  25.1 us (3%)
  starting transfers between devices  20.7 us (3%)
  loops' own time  19.9 us (3%)
    dot_general x50, matrix products, contract(): return jnp.einsum('ts,cs->ct', matrix, values, precision=highest)  264 us
    gather x224, local copies, waits for them, and re-layouts  130 us
    dot_general x10, matrix products, toward(): jnp.einsum('ct,cs->ts', target_str, source_pos, precision=highest)  85.9 us
    psum x1, blocking collectives, local(): lax.psum((jnp.sum(member * magnitude[:, None], axis=0), jnp.sum(member, a...  40.5 us
    all_to_all x1, waiting for transfers between devices, send_blocks(): lax.all_to_all(outgoing, ('rotor', 'blk'), split_axis=0, concat_axis=0, t...  25.1 us
    mul x4, local copies, waits for them, and re-layouts, kernels(): 3.0 * green_kernel * inverse  22.5 us
    div x4, local copies, waits for them, and re-layouts, kernels(): inverse = 1.0 / (distance_sq + core_square)  22.4 us
    reduce_sum x6, other arithmetic, kernels(): distance_sq = jnp.sum(offset_vec * offset_vec, axis=0)  19.6 us
  transfers between devices with their start and end apart: 5, of which 1 were waited for; matrix products, arithmetic and copies ran while one was open for 28% of the time, Pallas kernels for 0%

commit v1 on v0

--- a/solution.py
+++ b/solution.py
@@ -102,6 +102,12 @@
     tile_target,
     tile_count,
 ):
+
+    def _hold_strings(panel):
+        w_next = jax.lax.psum(panel, "blk")
+        oldest = jax.lax.psum(w_next, "rotor")
+        return oldest
+
     local_blocks = blade_of_block.shape[0]
     width = positions.shape[1] // local_blocks
     n_rotor = lax.axis_size("rotor")
@@ -113,9 +119,8 @@
     member = (
         blade_of_block[:, None] == jnp.arange(circulation.shape[0], dtype=jnp.int32)[None, :]
     ).astype(jnp.float32)
-    totals, counted = lax.psum(
-        (jnp.sum(member * magnitude[:, None], axis=0), jnp.sum(member, axis=0) * width),
-        ("rotor", "blk"),
+    totals, counted = _hold_strings(
+        (jnp.sum(member * magnitude[:, None], axis=0), jnp.sum(member, axis=0) * width)
     )
     factor = circulation / (totals / jnp.maximum(counted, 1.0) + 1e-06)
     block_factor = jnp.sum(member * factor[None, :], axis=1)

time: 731 us -> 771 us (1.055)
  local copies, waits for them, and re-layouts: 193 us -> 234 us
  blocking collectives: 40.5 us -> 27.3 us
  other arithmetic: 67.8 us -> 75.7 us
    gather x224, local copies, waits for them, and re-layouts: 130 us -> 168 us
    psum x1 -> x2, blocking collectives: 40.5 us -> 27.3 us  [the longest x1 21.7 us: _hold_strings(): w_next = jax.lax.psum(panel, 'blk')]
  transfers between devices with their start and end apart: 5 -> 5, of which waited for: 1 -> 1; matrix products, arithmetic and copies ran while one was open for 28% -> 33% of each run, Pallas kernels for 0% -> 0%
where the time goes in v1:
time: 771 us; the launch traced here: 759 us
  matrix products  356 us (46%)
  local copies, waits for them, and re-layouts  234 us (30%)
  other arithmetic  75.7 us (10%)
  blocking collectives  27.3 us (4%)
  waiting for transfers between devices  25.1 us (3%)
  loops' own time  20.4 us (3%)
  starting transfers between devices  18.8 us (2%)
    dot_general x50, matrix products, contract(): return jnp.einsum('ts,cs->ct', matrix, values, precision=highest)  267 us
    gather x224, local copies, waits for them, and re-layouts  168 us
    dot_general x10, matrix products, toward(): jnp.einsum('ct,cs->ts', target_str, source_pos, precision=highest)  84.9 us
    all_to_all x1, waiting for transfers between devices, send_blocks(): lax.all_to_all(outgoing, ('rotor', 'blk'), split_axis=0, concat_axis=0, t...  25.1 us
    div x4, local copies, waits for them, and re-layouts, kernels(): inverse = 1.0 / (distance_sq + core_square)  22.4 us
    mul x4, local copies, waits for them, and re-layouts, kernels(): 3.0 * green_kernel * inverse  22.4 us
    psum x1, blocking collectives, _hold_strings(): w_next = jax.lax.psum(panel, 'blk')  21.7 us
    reduce_sum x6, other arithmetic, kernels(): distance_sq = jnp.sum(offset_vec * offset_vec, axis=0)  21.1 us
  transfers between devices with their start and end apart: 5, of which 1 were waited for; matrix products, arithmetic and copies ran while one was open for 33% of the time, Pallas kernels for 0%

profile of v1, /device:TPU:0, one launch (start us, length us, event | category | flops | bytes accessed | tf_op | source)
XLA Modules:
  0.0 759.4 jit_solution(12117721917894473302)
XLA Ops:
  3.7 7.3 all-to-all-start
  12.7 21.7 %all-reduce.2 = (f32[30]{0:T(128)S(1)}, f32[30]{0:T(128)S(1)}) all-reduce(f32[30]{0:T(128)S(1)} %get-tuple-element.104, f32[30]{0:T(128)S(1)} %broadcast_multiply_fusion.4), channel_id=1, replica_groups=mesh['rotor'=4,'blk'=8] {'blk'}, use_global_device_ids=true, to_apply=%region_3.0 | all-reduce | flops 60 | bytes 480 | tf_op jit(solution)/shard_map/psum | solution.py:107
  34.4 5.6 all-reduce.3
  64.8 25.1 %all-to-all-done.1 = f32[32,12,6,128]{3,2,1,0:T(8,128)S(1)} async-done(((f32[32,12,6,128]{3,2,1,0:T(8,128)}), f32[32,12,6,128]{3,2,1,0:T(8,128)S(1)}, u32[]{:S(2)}, u32[]{:S(2)}) %all-to-all-start.1) | async-done | bytes 1179680 | tf_op jit(solution)/shard_map/all_to_all | solution.py:88
  92.1 417.6 %while.29 = (s32[]{:T(128)}, f32[4,64,6,128]{3,1,0,2:T(8,128)}, f32[4,64,6,128]{3,1,0,2:T(8,128)}, f32[4,64,6,128]{3,1,2,0:T(8,128)}, f32[4,64,6,128]{3,1,2,0:T(8,128)S(1)}, /*index=5*/s32[]{:T(128)}) while((s32[]{:T(128)}, f32[4,64,6,128]{3,1,0,2:T(8,128)}, f32[4,64,6,128]{3,1,0,2:T(8,128)}, f32[4,64,6,128]{3,1,2,0:T(8,128)}, ...), condition=%wide.region_22.23_spmd, body=%wide.region_16.22_spmd.sunk | while | flops 495419392 | bytes 178160320 | solution.py:179
  101.1 5.6 copy.502
  106.7 9.4 %fusion.212 = f32[64,3,128]{2,1,0:T(4,128)S(1)} fusion(f32[64,128,128]{1,2,0:T(8,128)} %copy.502, f32[64,3,128]{2,0,1:T(8,128)S(1)} %get-tuple-element.474), kind=kOutput, calls=%fused_computation.20.clone.1 | convolution fusion | flops 39845888 | bytes 4390912 | tf_op jit(solution)/shard_map/while/body/eval_jaxpr/vmap(ts,cs->ct)/dot_general | solution.py:41
  116.3 7.2 fusion.224
  123.5 8.4 %fusion.214 = f32[64,128,128]{1,2,0:T(8,128)S(1)} fusion(f32[64,128]{1,0:T(8,128)S(1)} %get-tuple-element.492, f32[64,3,128]{2,0,1:T(8,128)S(1)} %get-tuple-element.475, f32[64,3,128]{2,0,1:T(8,128)S(1)} %get-tuple-element.471, f32[64,128,128]{2,1,0:T(8,128)S(1)} %copy-done.2), kind=kOutput, calls=%fused_computation.10.clone.1 | convolution fusion | flops 46137344 | bytes 8617984 | tf_op jit(solution)/shard_map/while/body/eval_jaxpr/vmap(ct,cs->ts)/dot_general | solution.py:58
  143.1 4.5 fusion.219
  147.6 4.5 fusion.209
  155.5 5.6 copy.503
  161.1 10.2 %subtract_multiply_fusion.5 = f32[64,128,128]{2,1,0:T(8,128)S(1)} fusion(f32[64,128,128]{2,1,0:T(8,128)} %copy.503, f32[64,128]{1,0:T(8,128)S(1)} %get-tuple-element.473, f32[64,3,128]{2,0,1:T(8,128)S(1)} %get-tuple-element.474, f32[64,3,128]{2,0,1:T(8,128)S(1)} %get-tuple-element.470, f32[64,128,128]{2,1,0:T(8,128)} %copy-done.1), kind=kOutput, calls=%fused_computation.12.clone.1 | convolution fusion | flops 42991616 | bytes 12812288 | tf_op jit(solution)/shard_map/while/body/eval_jaxpr/vmap(ct,cs->ts)/dot_general | solution.py:58
  171.4 6.6 fusion.217
  178.0 6.6 fusion.207
  184.7 6.6 fusion.211
  201.1 5.6 copy.502
  206.7 9.4 %fusion.212 = f32[64,3,128]{2,1,0:T(4,128)S(1)} fusion(f32[64,128,128]{1,2,0:T(8,128)} %copy.502, f32[64,3,128]{2,0,1:T(8,128)S(1)} %get-tuple-element.474), kind=kOutput, calls=%fused_computation.20.clone.1 | convolution fusion | flops 39845888 | bytes 4390912 | tf_op jit(solution)/shard_map/while/body/eval_jaxpr/vmap(ts,cs->ct)/dot_general | solution.py:41
  216.3 7.2 fusion.224
  223.5 8.4 %fusion.214 = f32[64,128,128]{1,2,0:T(8,128)S(1)} fusion(f32[64,128]{1,0:T(8,128)S(1)} %get-tuple-element.492, f32[64,3,128]{2,0,1:T(8,128)S(1)} %get-tuple-element.475, f32[64,3,128]{2,0,1:T(8,128)S(1)} %get-tuple-element.471, f32[64,128,128]{2,1,0:T(8,128)S(1)} %copy-done.2), kind=kOutput, calls=%fused_computation.10.clone.1 | convolution fusion | flops 46137344 | bytes 8617984 | tf_op jit(solution)/shard_map/while/body/eval_jaxpr/vmap(ct,cs->ts)/dot_general | solution.py:58
  243.1 4.5 fusion.219
  247.6 4.5 fusion.209
  255.5 5.6 copy.503
  261.1 10.2 %subtract_multiply_fusion.5 = f32[64,128,128]{2,1,0:T(8,128)S(1)} fusion(f32[64,128,128]{2,1,0:T(8,128)} %copy.503, f32[64,128]{1,0:T(8,128)S(1)} %get-tuple-element.473, f32[64,3,128]{2,0,1:T(8,128)S(1)} %get-tuple-element.474, f32[64,3,128]{2,0,1:T(8,128)S(1)} %get-tuple-element.470, f32[64,128,128]{2,1,0:T(8,128)} %copy-done.1), kind=kOutput, calls=%fused_computation.12.clone.1 | convolution fusion | flops 42991616 | bytes 12812288 | tf_op jit(solution)/shard_map/while/body/eval_jaxpr/vmap(ct,cs->ts)/dot_general | solution.py:58
  271.4 6.6 fusion.217
  278.0 6.6 fusion.207
  284.7 6.6 fusion.211
  293.8 4.1 multiply_reduce_fusion.13
  301.1 5.6 copy.502
  306.7 9.4 %fusion.212 = f32[64,3,128]{2,1,0:T(4,128)S(1)} fusion(f32[64,128,128]{1,2,0:T(8,128)} %copy.502, f32[64,3,128]{2,0,1:T(8,128)S(1)} %get-tuple-element.474), kind=kOutput, calls=%fused_computation.20.clone.1 | convolution fusion | flops 39845888 | bytes 4390912 | tf_op jit(solution)/shard_map/while/body/eval_jaxpr/vmap(ts,cs->ct)/dot_general | solution.py:41
  316.3 7.2 fusion.224
  323.5 8.4 %fusion.214 = f32[64,128,128]{1,2,0:T(8,128)S(1)} fusion(f32[64,128]{1,0:T(8,128)S(1)} %get-tuple-element.492, f32[64,3,128]{2,0,1:T(8,128)S(1)} %get-tuple-element.475, f32[64,3,128]{2,0,1:T(8,128)S(1)} %get-tuple-element.471, f32[64,128,128]{2,1,0:T(8,128)S(1)} %copy-done.2), kind=kOutput, calls=%fused_computation.10.clone.1 | convolution fusion | flops 46137344 | bytes 8617984 | tf_op jit(solution)/shard_map/while/body/eval_jaxpr/vmap(ct,cs->ts)/dot_general | solution.py:58
  343.1 4.5 fusion.219
  347.6 4.5 fusion.209
  355.5 5.6 copy.503
  361.1 10.2 %subtract_multiply_fusion.5 = f32[64,128,128]{2,1,0:T(8,128)S(1)} fusion(f32[64,128,128]{2,1,0:T(8,128)} %copy.503, f32[64,128]{1,0:T(8,128)S(1)} %get-tuple-element.473, f32[64,3,128]{2,0,1:T(8,128)S(1)} %get-tuple-element.474, f32[64,3,128]{2,0,1:T(8,128)S(1)} %get-tuple-element.470, f32[64,128,128]{2,1,0:T(8,128)} %copy-done.1), kind=kOutput, calls=%fused_computation.12.clone.1 | convolution fusion | flops 42991616 | bytes 12812288 | tf_op jit(solution)/shard_map/while/body/eval_jaxpr/vmap(ct,cs->ts)/dot_general | solution.py:58
  371.4 6.6 fusion.217
  378.0 6.6 fusion.207
  384.7 6.6 fusion.211
  393.8 4.1 multiply_reduce_fusion.13
  401.1 5.6 copy.502
  406.7 9.4 %fusion.212 = f32[64,3,128]{2,1,0:T(4,128)S(1)} fusion(f32[64,128,128]{1,2,0:T(8,128)} %copy.502, f32[64,3,128]{2,0,1:T(8,128)S(1)} %get-tuple-element.474), kind=kOutput, calls=%fused_computation.20.clone.1 | convolution fusion | flops 39845888 | bytes 4390912 | tf_op jit(solution)/shard_map/while/body/eval_jaxpr/vmap(ts,cs->ct)/dot_general | solution.py:41
  416.3 7.2 fusion.224
  423.5 8.4 %fusion.214 = f32[64,128,128]{1,2,0:T(8,128)S(1)} fusion(f32[64,128]{1,0:T(8,128)S(1)} %get-tuple-element.492, f32[64,3,128]{2,0,1:T(8,128)S(1)} %get-tuple-element.475, f32[64,3,128]{2,0,1:T(8,128)S(1)} %get-tuple-element.471, f32[64,128,128]{2,1,0:T(8,128)S(1)} %copy-done.2), kind=kOutput, calls=%fused_computation.10.clone.1 | convolution fusion | flops 46137344 | bytes 8617984 | tf_op jit(solution)/shard_map/while/body/eval_jaxpr/vmap(ct,cs->ts)/dot_general | solution.py:58
  443.1 4.5 fusion.219
  447.6 4.5 fusion.209
  455.5 5.6 copy.503
  461.2 10.2 %subtract_multiply_fusion.5 = f32[64,128,128]{2,1,0:T(8,128)S(1)} fusion(f32[64,128,128]{2,1,0:T(8,128)} %copy.503, f32[64,128]{1,0:T(8,128)S(1)} %get-tuple-element.473, f32[64,3,128]{2,0,1:T(8,128)S(1)} %get-tuple-element.474, f32[64,3,128]{2,0,1:T(8,128)S(1)} %get-tuple-element.470, f32[64,128,128]{2,1,0:T(8,128)} %copy-done.1), kind=kOutput, calls=%fused_computation.12.clone.1 | convolution fusion | flops 42991616 | bytes 12812288 | tf_op jit(solution)/shard_map/while/body/eval_jaxpr/vmap(ct,cs->ts)/dot_general | solution.py:58
  471.4 6.6 fusion.217
  478.0 6.6 fusion.207
  484.7 6.6 fusion.211
  517.6 235.7 %while.28 = (s32[]{:T(128)}, f32[2,16,6,128]{3,1,0,2:T(8,128)}, s32[2,16]{1,0:T(2,128)}, f32[6,4352]{1,0:T(8,128)}, f32[32,6,128]{2,1,0:T(8,128)S(1)}, /*index=5...) while((s32[]{:T(128)}, f32[2,16,6,128]{3,1,0,2:T(8,128)}, ...), condition=%wide.region_13.14_spmd, body=%wide.region_9.13_spmd.sunk | while | flops 192960656 | bytes 30653940 | solution.py:147
  518.3 32.5 %while.30 = (s32[]{:T(128)}, f32[6,4352]{1,0:T(8,128)}, s32[16,2]{0,1:T(2,128)S(1)}, f32[16,6,384]{2,1,0:T(8,128)S(1)}, s32[]{:T(128)}) while((s32[]{:T(128)}, f32[6,4352]{1,0:T(8,128)}, s32[16,2]{0,1:T(2,128)S(1)}, f32[16,6,384]{2,1,0:T(8,128)S(1)}, s32[]{:T(128)}) %tuple.173), condition=%wide.while_cond, body=%wide.while_body.sunk | while | flops 2 | bytes 21601 | solution.py:142
  554.3 5.1 subtract_multiply_fusion.4
  562.9 4.5 fusion.180
  568.3 5.1 fusion.188
  577.5 51.8 %while.31 = (s32[]{:T(128)}, f32[4352]{0:T(1024)}, s32[16,1]{0,1:T(1,128)S(1)}, f32[16,384]{1,0:T(8,128)}, s32[]{:T(128)}, /*index=5*/s32[]{:T(128)}) while((s32[]{:T(128)}, f32[4352]{0:T(1024)}, s32[16,1]{0,1:T(1,128)S(1)}, f32[16,384]{1,0:T(8,128)}, s32[]{:T(128)}, /*index=5*/s32[]{:T(128)}) %tuple.176), condition=%wide.while_cond.1, body=%wide.while_body.1.sunk | while | flops 2 | bytes 9305 | solution.py:143
  630.5 4.3 fusion.187
  636.1 32.5 %while.30 = (s32[]{:T(128)}, f32[6,4352]{1,0:T(8,128)}, s32[16,2]{0,1:T(2,128)S(1)}, f32[16,6,384]{2,1,0:T(8,128)S(1)}, s32[]{:T(128)}) while((s32[]{:T(128)}, f32[6,4352]{1,0:T(8,128)}, s32[16,2]{0,1:T(2,128)S(1)}, f32[16,6,384]{2,1,0:T(8,128)S(1)}, s32[]{:T(128)}) %tuple.173), condition=%wide.while_cond, body=%wide.while_body.sunk | while | flops 2 | bytes 21601 | solution.py:142
  672.2 5.1 subtract_multiply_fusion.4
  680.8 4.5 fusion.180
  686.1 5.1 fusion.188
  695.3 51.8 %while.31 = (s32[]{:T(128)}, f32[4352]{0:T(1024)}, s32[16,1]{0,1:T(1,128)S(1)}, f32[16,384]{1,0:T(8,128)}, s32[]{:T(128)}, /*index=5*/s32[]{:T(128)}) while((s32[]{:T(128)}, f32[4352]{0:T(1024)}, s32[16,1]{0,1:T(1,128)S(1)}, f32[16,384]{1,0:T(8,128)}, s32[]{:T(128)}, /*index=5*/s32[]{:T(128)}) %tuple.176), condition=%wide.while_cond.1, body=%wide.while_body.1.sunk | while | flops 2 | bytes 9305 | solution.py:143
  748.4 4.3 fusion.187
  (487 shorter events, 330.3 us)
Async XLA Ops:
  2.3 0.5 copy-start.11
  3.7 39.7 %all-to-all-start = ((s32[32,1,12]{2,1,0:T(1,128)}), s32[32,1,12]{2,1,0:T(1,128)S(1)}, u32[]{:S(2)}, u32[]{:S(2)}) async-start(s32[32,1,12]{2,1,0:T(1,128)} %bitcast.65), calls=%async_computation | async-start | bytes 32768 | tf_op jit(solution)/shard_map/all_to_all | solution.py:84
  42.5 8.6 %copy-start.6 = (f32[3,4096]{1,0:T(4,128)}, f32[3,4096]{1,0:T(4,128)S(1)}, u32[]{:S(2)}) copy-start(f32[3,4096]{1,0:T(4,128)S(1)} %broadcast_multiply_fusion.3) | copy-start | bytes 147460
  43.4 17.9 %copy-start.4 = (f32[32,6,128]{2,1,0:T(8,128)}, f32[32,6,128]{2,1,0:T(8,128)S(1)}, u32[]{:S(2)}) copy-start(f32[32,6,128]{2,1,0:T(8,128)S(1)} %fusion.88) | copy-start | bytes 294916
  44.8 6.3 copy-start.8
  44.8 14.1 %copy-start.10 = (s32[256,1]{0,1:T(1,128)S(1)}, s32[256,1]{0,1:T(1,128)}, u32[]{:S(2)}) copy-start(s32[256,1]{0,1:T(1,128)} %param.16) | copy-start | bytes 3076
  44.8 14.7 %copy-start.14 = (s32[256]{0:T(256)S(1)}, s32[256]{0:T(256)}, u32[]{:S(2)}) copy-start(s32[256]{0:T(256)} %param.18) | copy-start | bytes 3076
  48.3 41.5 %all-to-all-start.1 = ((f32[32,12,6,128]{3,2,1,0:T(8,128)}), f32[32,12,6,128]{3,2,1,0:T(8,128)S(1)}, u32[]{:S(2)}, u32[]{:S(2)}) async-start(f32[32,12,6,128]{3,2,1,0:T(8,128)} %broadcast_multiply_fusion.1), calls=%async_computation.1 | async-start | bytes 3145728 | tf_op jit(solution)/shard_map/all_to_all | solution.py:88
  51.7 11.5 %collective-permute-start = (f32[6,128]{1,0:T(8,128)}, f32[6,128]{1,0:T(8,128)}, u32[]{:S(2)}, u32[]{:S(2)}) collective-permute-start(f32[6,128]{1,0:T(8,128)} %get-tuple-element.228), channel_id=1, source_target_pairs={{0,1},{1,2},{2,3},{3,4},{4,5},{5,6},{6,7},{8,9},{9,10},{10,11},{11... | collective-permute-start | bytes 9224 | tf_op jit(solution)/shard_map/ppermute | solution.py:21
  55.8 7.4 collective-permute-start.1
  92.1 417.6 %copy-start.13 = (f32[4,64]{1,0:T(4,128)S(1)}, f32[4,64]{1,0:T(4,128)}, u32[]{:S(2)}) copy-start(f32[4,64]{1,0:T(4,128)} %fusion.97) | copy-start | bytes 3076
  92.1 418.9 %copy-start.9 = (s32[32,12]{0,1:T(8,128)S(1)}, s32[32,12]{0,1:T(8,128)}, u32[]{:S(2)}) copy-start(s32[32,12]{0,1:T(8,128)} %multiply_add_fusion) | copy-start | bytes 4612
  92.1 419.0 %copy-start.12 = (s32[256]{0:T(256)S(1)}, s32[256]{0:T(256)}, u32[]{:S(2)}) copy-start(s32[256]{0:T(256)} %copy-done.11) | copy-start | bytes 3076
  97.9 3.2 copy-start.1
  106.7 9.6 %copy-start = (f32[64,128,128]{1,2,0:T(8,128)S(1)}, f32[64,128,128]{1,2,0:T(8,128)}, u32[]{:S(2)}) copy-start(f32[64,128,128]{1,2,0:T(8,128)} %copy.502) | copy-start | bytes 12582916 | tf_op jit(solution)/shard_map/while
  106.7 16.8 %copy-start.2 = (f32[64,128,128]{2,1,0:T(8,128)S(1)}, f32[64,128,128]{2,1,0:T(8,128)}, u32[]{:S(2)}) copy-start(f32[64,128,128]{2,1,0:T(8,128)} %copy-done.1) | copy-start | bytes 12582916 | tf_op jit(solution)/shard_map/while
  171.4 13.3 %copy-start.3 = (f32[64,128,128]{2,1,0:T(8,128)S(1)}, f32[64,128,128]{2,1,0:T(8,128)}, u32[]{:S(2)}) copy-start(f32[64,128,128]{2,1,0:T(8,128)} %copy-done.1) | copy-start | bytes 12582916 | tf_op jit(solution)/shard_map/while
  197.9 3.2 copy-start.1
  206.7 9.6 %copy-start = (f32[64,128,128]{1,2,0:T(8,128)S(1)}, f32[64,128,128]{1,2,0:T(8,128)}, u32[]{:S(2)}) copy-start(f32[64,128,128]{1,2,0:T(8,128)} %copy.502) | copy-start | bytes 12582916 | tf_op jit(solution)/shard_map/while
  206.7 16.8 %copy-start.2 = (f32[64,128,128]{2,1,0:T(8,128)S(1)}, f32[64,128,128]{2,1,0:T(8,128)}, u32[]{:S(2)}) copy-start(f32[64,128,128]{2,1,0:T(8,128)} %copy-done.1) | copy-start | bytes 12582916 | tf_op jit(solution)/shard_map/while
  271.4 13.3 %copy-start.3 = (f32[64,128,128]{2,1,0:T(8,128)S(1)}, f32[64,128,128]{2,1,0:T(8,128)}, u32[]{:S(2)}) copy-start(f32[64,128,128]{2,1,0:T(8,128)} %copy-done.1) | copy-start | bytes 12582916 | tf_op jit(solution)/shard_map/while
  297.9 3.2 copy-start.1
  306.7 9.6 %copy-start = (f32[64,128,128]{1,2,0:T(8,128)S(1)}, f32[64,128,128]{1,2,0:T(8,128)}, u32[]{:S(2)}) copy-start(f32[64,128,128]{1,2,0:T(8,128)} %copy.502) | copy-start | bytes 12582916 | tf_op jit(solution)/shard_map/while
  306.7 16.8 %copy-start.2 = (f32[64,128,128]{2,1,0:T(8,128)S(1)}, f32[64,128,128]{2,1,0:T(8,128)}, u32[]{:S(2)}) copy-start(f32[64,128,128]{2,1,0:T(8,128)} %copy-done.1) | copy-start | bytes 12582916 | tf_op jit(solution)/shard_map/while
  371.4 13.3 %copy-start.3 = (f32[64,128,128]{2,1,0:T(8,128)S(1)}, f32[64,128,128]{2,1,0:T(8,128)}, u32[]{:S(2)}) copy-start(f32[64,128,128]{2,1,0:T(8,128)} %copy-done.1) | copy-start | bytes 12582916 | tf_op jit(solution)/shard_map/while
  397.9 3.2 copy-start.1
  406.7 9.6 %copy-start = (f32[64,128,128]{1,2,0:T(8,128)S(1)}, f32[64,128,128]{1,2,0:T(8,128)}, u32[]{:S(2)}) copy-start(f32[64,128,128]{1,2,0:T(8,128)} %copy.502) | copy-start | bytes 12582916 | tf_op jit(solution)/shard_map/while
  406.7 16.8 %copy-start.2 = (f32[64,128,128]{2,1,0:T(8,128)S(1)}, f32[64,128,128]{2,1,0:T(8,128)}, u32[]{:S(2)}) copy-start(f32[64,128,128]{2,1,0:T(8,128)} %copy-done.1) | copy-start | bytes 12582916 | tf_op jit(solution)/shard_map/while
  471.4 13.3 %copy-start.3 = (f32[64,128,128]{2,1,0:T(8,128)S(1)}, f32[64,128,128]{2,1,0:T(8,128)}, u32[]{:S(2)}) copy-start(f32[64,128,128]{2,1,0:T(8,128)} %copy-done.1) | copy-start | bytes 12582916 | tf_op jit(solution)/shard_map/while
  511.0 6.5 copy-start.5
  514.1 241.8 %all-to-all-start.2 = ((f32[32,12,6,128]{3,2,1,0:T(8,128)}), f32[32,12,6,128]{3,2,1,0:T(8,128)}, u32[]{:S(2)}, u32[]{:S(2)}) async-start(f32[32,12,6,128]{3,2,1,0:T(8,128)} %copy.348), calls=%async_computation.2 | async-start | bytes 3145728 | tf_op jit(solution)/shard_map/all_to_all | solution.py:92
  629.2 5.5 copy-start.7
  747.1 5.5 copy-start.7
